TPU v7x, 32 devices: a whole 2x2x4 slice. The times are simulated.
32 devices in a mesh: fsdp: 8 (over z, x), rep: 4 (over y, core).
Axes of the slice: x: 2, y: 2, z: 4, core: 2. Of those that a mesh axis runs over, the one named last changes fastest.
Arguments:
- layer_input: bfloat16 [32768, 768], P(('fsdp', 'rep')), may hold values from -6 to 6
- qkv_weight: bfloat16 [768, 2304], P('fsdp'), may hold values from -0.21875 to 0.21875
- attn_weight: bfloat16 [768, 768], P('fsdp'), may hold values from -1.75 to 1.75
- wide_weight: bfloat16 [768, 2304], P('fsdp'), may hold values from -0.21875 to 0.21875
- narrow_weight: bfloat16 [768, 1152], P('fsdp'), may hold values from -0.375 to 0.375
- first_gain: bfloat16 [768], P('fsdp'), may hold values from 0.099609375 to 1.8984375
- second_gain: bfloat16 [768], P('fsdp'), may hold values from 0.099609375 to 1.8984375
- out_grad: bfloat16 [32768, 768], P(('fsdp', 'rep')), may hold values from -12 to 12
- token_seg: int32 [32768], P(('fsdp', 'rep')), may hold values from 0 to 255, as said below
- token_live: int32 [32768], P(('fsdp', 'rep')), may hold values from 0 to 1, as said below
Outputs:
- layer_output: bfloat16 [32768, 768], P(('fsdp', 'rep'))
- input_grad: float32 [32768, 768], P(('fsdp', 'rep'))
- qkv_grad: float32 [768, 2304], P('fsdp')
- attn_grad: float32 [768, 768], P('fsdp')
- wide_grad: float32 [768, 2304], P('fsdp')
- narrow_grad: float32 [768, 1152], P('fsdp')
- first_grad: float32 [768], P('fsdp')
- second_grad: float32 [768], P('fsdp')
Inputs may be any that keep to these rules, and one draw needn't show every extreme that they name: `token_seg`: numbers never fall along the slots; all slots of one number lie in one block of 1024 slots (one device's), and each number begins at a multiple of 128; every block begins a new number; the last tile of the last block begins a number of its own. `token_live`: within each number of token_seg the live slots come first and its first slot is live; in every draw one block of 1024 slots holds a single number with every slot live.
All inputs are finite; a program needn't handle non-finite values.
Results may differ from a plain program's by a relative error of at most 0.018.
Values may be sent and summed in bfloat16 or wider, within the bound.
A program may use at most 320 MiB of HBM per device.

v0:
```python
import math
import jax
import jax.numpy as jnp
from jax import lax
from jax.sharding import PartitionSpec as P

HDIM = 64
TILE = 128
QBLOCK = 512
rope_base = 160000.0
eps = 1e-05
masked_score = -1e30


def layer_norm(values, scales):
    center = values - jnp.mean(values, axis=-1, keepdims=True)
    spread = jnp.mean(center * center, axis=-1, keepdims=True)
    return center * lax.rsqrt(spread + eps) * scales


def rope_tables(seg_rows):
    length = seg_rows.shape[0]
    firsts = seg_rows[::TILE]
    before = jnp.sum((firsts[None, :] < seg_rows[:, None]).astype(jnp.int32), axis=1)
    places = jnp.arange(length, dtype=jnp.int32) - TILE * before
    freq_index = jnp.arange(HDIM // 2, dtype=jnp.float32)
    inverse = jnp.exp(freq_index * (-2.0 * math.log(rope_base) / HDIM))
    angles = places.astype(jnp.float32)[:, None] * inverse[None, :]
    angles = jnp.concatenate([angles, angles], axis=1)
    return (jnp.cos(angles)[:, None, :], jnp.sin(angles)[:, None, :])


def rotate(values, cos_tab, sin_tab):
    half_dim = values.shape[-1] // 2
    turned = jnp.concatenate([-values[..., half_dim:], values[..., :half_dim]], axis=-1)
    return values * cos_tab + turned * sin_tab


def rotate_back(grads, cos_tab, sin_tab):
    half_dim = grads.shape[-1] // 2
    sined = grads * sin_tab
    return grads * cos_tab + jnp.concatenate(
        [sined[..., half_dim:], -sined[..., :half_dim]], axis=-1
    )


def geglu(lifted):
    half_ff = lifted.shape[1] // 2
    return jax.nn.gelu(lifted[:, :half_ff], approximate=False) * lifted[:, half_ff:]


def block_scores(query_rows, keyset, seg_rows, token_seg, live_keys, scaling):
    raw = (
        jnp.einsum("qhd,khd->hqk", query_rows, keyset, preferred_element_type=jnp.float32) * scaling
    )
    allowed = (seg_rows[:, None] == token_seg[None, :]) & live_keys[None, :]
    return jnp.where(allowed[None], raw, masked_score)


def on_device(
    layer_input,
    qkv_weight,
    attn_weight,
    wide_weight,
    narrow_weight,
    first_gain,
    second_gain,
    out_grad,
    token_seg,
    token_live,
):
    length = layer_input.shape[0]
    model_width = layer_input.shape[1]
    head_count = model_width // HDIM
    scaling = 1.0 / math.sqrt(HDIM)
    qkv_full, attn_full, wide_full, narrow_full, gain_one, gain_two = (
        lax.all_gather(qkv_weight, "fsdp", axis=0, tiled=True),
        lax.all_gather(attn_weight, "fsdp", axis=0, tiled=True),
        lax.all_gather(wide_weight, "fsdp", axis=0, tiled=True),
        lax.all_gather(narrow_weight, "fsdp", axis=0, tiled=True),
        lax.all_gather(first_gain, "fsdp", axis=0, tiled=True),
        lax.all_gather(second_gain, "fsdp", axis=0, tiled=True),
    )
    scale_one = gain_one.astype(jnp.float32)
    scale_two = gain_two.astype(jnp.float32)
    residual_in = layer_input.astype(jnp.float32)
    live_keys = token_live > 0
    cos_tab, sin_tab = rope_tables(token_seg)
    normed_one = layer_norm(residual_in, scale_one).astype(jnp.bfloat16)
    packed = jnp.dot(normed_one, qkv_full, preferred_element_type=jnp.float32)
    queries = rotate(
        packed[:, :model_width].reshape(length, head_count, HDIM), cos_tab, sin_tab
    ).astype(jnp.bfloat16)
    keyset = rotate(
        packed[:, model_width : 2 * model_width].reshape(length, head_count, HDIM), cos_tab, sin_tab
    ).astype(jnp.bfloat16)
    valueset = packed[:, 2 * model_width :].reshape(length, head_count, HDIM).astype(jnp.bfloat16)
    mixed_list = []
    lse_list = []
    for begin_row in range(0, length, QBLOCK):
        seg_rows = token_seg[begin_row : begin_row + QBLOCK]
        scores = block_scores(
            queries[begin_row : begin_row + QBLOCK], keyset, seg_rows, token_seg, live_keys, scaling
        )
        top_score = jnp.max(scores, axis=-1, keepdims=True)
        expo = jnp.exp(scores - top_score)
        total = jnp.sum(expo, axis=-1, keepdims=True)
        probs = (expo / total).astype(jnp.bfloat16)
        lse_list.append(top_score + jnp.log(total))
        block_out = jnp.einsum("hqk,khd->qhd", probs, valueset, preferred_element_type=jnp.float32)
        mixed_list.append(block_out.reshape(QBLOCK, model_width).astype(jnp.bfloat16))
    mixed_rows = jnp.concatenate(mixed_list, axis=0)
    middle = residual_in + jnp.dot(mixed_rows, attn_full, preferred_element_type=jnp.float32)
    normed_two = layer_norm(middle, scale_two).astype(jnp.bfloat16)
    lifted = jnp.dot(normed_two, wide_full, preferred_element_type=jnp.float32)
    hidden = geglu(lifted).astype(jnp.bfloat16)
    layer_out = middle + jnp.einsum(
        "tf,df->td", hidden, narrow_full, preferred_element_type=jnp.float32
    )
    qkv_full, attn_full, wide_full, narrow_full, gain_one, gain_two = (
        lax.all_gather(qkv_weight, "fsdp", axis=0, tiled=True),
        lax.all_gather(attn_weight, "fsdp", axis=0, tiled=True),
        lax.all_gather(wide_weight, "fsdp", axis=0, tiled=True),
        lax.all_gather(narrow_weight, "fsdp", axis=0, tiled=True),
        lax.all_gather(first_gain, "fsdp", axis=0, tiled=True),
        lax.all_gather(second_gain, "fsdp", axis=0, tiled=True),
    )
    scale_one = gain_one.astype(jnp.float32)
    scale_two = gain_two.astype(jnp.float32)
    grad_top = out_grad.astype(jnp.float32) * token_live.astype(jnp.float32)[:, None]
    grad_top_low = grad_top.astype(jnp.bfloat16)
    narrow_term = jnp.einsum("td,tf->df", grad_top_low, hidden, preferred_element_type=jnp.float32)
    grad_hidden = jnp.dot(grad_top_low, narrow_full, preferred_element_type=jnp.float32)
    _, pull_gate = jax.vjp(geglu, lifted)
    grad_lifted = pull_gate(grad_hidden)[0].astype(jnp.bfloat16)
    wide_term = jnp.einsum("td,tf->df", normed_two, grad_lifted, preferred_element_type=jnp.float32)
    grad_norm_two = jnp.einsum(
        "tf,df->td", grad_lifted, wide_full, preferred_element_type=jnp.float32
    )
    _, pull_two = jax.vjp(layer_norm, middle, scale_two)
    grad_mid_ln, second_term = pull_two(grad_norm_two)
    grad_middle = grad_top + grad_mid_ln
    grad_middle_low = grad_middle.astype(jnp.bfloat16)
    attn_term = jnp.einsum(
        "td,te->de", mixed_rows, grad_middle_low, preferred_element_type=jnp.float32
    )
    grad_mixed = jnp.einsum(
        "te,de->td", grad_middle_low, attn_full, preferred_element_type=jnp.float32
    )
    grad_mixed = grad_mixed.astype(jnp.bfloat16).reshape(length, head_count, HDIM)
    grad_keys = jnp.zeros((length, head_count, HDIM), jnp.float32)
    grad_values = jnp.zeros((length, head_count, HDIM), jnp.float32)
    grad_query_list = []
    for block_index, begin_row in enumerate(range(0, length, QBLOCK)):
        seg_rows = token_seg[begin_row : begin_row + QBLOCK]
        query_rows = queries[begin_row : begin_row + QBLOCK]
        grad_rows = grad_mixed[begin_row : begin_row + QBLOCK]
        scores = block_scores(query_rows, keyset, seg_rows, token_seg, live_keys, scaling)
        probs_f32 = jnp.exp(scores - lse_list[block_index])
        probs_low = probs_f32.astype(jnp.bfloat16)
        grad_values = grad_values + jnp.einsum(
            "hqk,qhd->khd", probs_low, grad_rows, preferred_element_type=jnp.float32
        )
        grad_probs = jnp.einsum(
            "qhd,khd->hqk", grad_rows, valueset, preferred_element_type=jnp.float32
        )
        row_delta = jnp.sum(probs_f32 * grad_probs, axis=-1, keepdims=True)
        grad_scores = (probs_f32 * (grad_probs - row_delta)).astype(jnp.bfloat16)
        grad_query_list.append(
            jnp.einsum("hqk,khd->qhd", grad_scores, keyset, preferred_element_type=jnp.float32)
            * scaling
        )
        grad_keys = (
            grad_keys
            + jnp.einsum(
                "hqk,qhd->khd", grad_scores, query_rows, preferred_element_type=jnp.float32
            )
            * scaling
        )
    grad_queries = jnp.concatenate(grad_query_list, axis=0)
    grad_packed = jnp.concatenate(
        [
            rotate_back(grad_queries, cos_tab, sin_tab).reshape(length, model_width),
            rotate_back(grad_keys, cos_tab, sin_tab).reshape(length, model_width),
            grad_values.reshape(length, model_width),
        ],
        axis=1,
    ).astype(jnp.bfloat16)
    qkv_term = jnp.einsum("td,tf->df", normed_one, grad_packed, preferred_element_type=jnp.float32)
    grad_norm_one = jnp.einsum(
        "tf,df->td", grad_packed, qkv_full, preferred_element_type=jnp.float32
    )
    _, pull_one = jax.vjp(layer_norm, residual_in, scale_one)
    grad_in_ln, first_term = pull_one(grad_norm_one)
    input_grad = grad_middle + grad_in_ln
    shares = (
        lax.psum_scatter(qkv_term, "fsdp", scatter_dimension=0, tiled=True),
        lax.psum_scatter(attn_term, "fsdp", scatter_dimension=0, tiled=True),
        lax.psum_scatter(wide_term, "fsdp", scatter_dimension=0, tiled=True),
        lax.psum_scatter(narrow_term, "fsdp", scatter_dimension=0, tiled=True),
        lax.psum_scatter(first_term, "fsdp", scatter_dimension=0, tiled=True),
        lax.psum_scatter(second_term, "fsdp", scatter_dimension=0, tiled=True),
    )
    shares = (
        lax.psum(shares[0].astype(jnp.bfloat16), "rep").astype(jnp.float32),
        lax.psum(shares[1].astype(jnp.bfloat16), "rep").astype(jnp.float32),
        lax.psum(shares[2].astype(jnp.bfloat16), "rep").astype(jnp.float32),
        lax.psum(shares[3].astype(jnp.bfloat16), "rep").astype(jnp.float32),
        lax.psum(shares[4].astype(jnp.bfloat16), "rep").astype(jnp.float32),
        lax.psum(shares[5].astype(jnp.bfloat16), "rep").astype(jnp.float32),
    )
    return (
        layer_out.astype(jnp.bfloat16),
        input_grad,
        shares[0],
        shares[1],
        shares[2],
        shares[3],
        shares[4],
        shares[5],
    )


def solution(mesh):
    return jax.shard_map(
        on_device,
        mesh=mesh,
        in_specs=(
            P(("fsdp", "rep"), None),
            P("fsdp", None),
            P("fsdp", None),
            P("fsdp", None),
            P("fsdp", None),
            P("fsdp"),
            P("fsdp"),
            P(("fsdp", "rep"), None),
            P(("fsdp", "rep")),
            P(("fsdp", "rep")),
        ),
        out_specs=(
            P(("fsdp", "rep"), None),
            P(("fsdp", "rep"), None),
            P("fsdp", None),
            P("fsdp", None),
            P("fsdp", None),
            P("fsdp", None),
            P("fsdp"),
            P("fsdp"),
        ),
        check_vma=False,
    )
```

profile of v0, /device:TPU:0, one launch (start us, length us, event | category | flops | bytes accessed | tf_op | source)
XLA Modules:
  0.0 737.4 jit_solution(18001098060533873576)
XLA Ops:
  13.6 1.3 fusion.91
  17.2 23.5 %all-reduce.7 = (bf16[768]{0:T(1024)(128)(2,1)S(1)}, bf16[768]{0:T(1024)(128)(2,1)S(1)}) all-reduce(bf16[768]{0:T(1024)(128)(2,1)S(1)} %dynamic-update-slice, bf16[768]{0:T(1024)(128)(2,1)S(1)} %dynamic-update-slice.1), channel_id=1, replica_groups=mesh['fsdp'=8,'rep'=4] {'fsdp'}, use_global_device_ids=true, to_apply=%add.2 | all-reduce | flops 1536 | bytes 6144
  42.2 1.7 broadcast_multiply_fusion.1
  46.7 1.6 copy.54
  48.3 1.7 compare_and_fusion.1
  50.0 28.4 %all-gather.5.cloned.1.call-done = bf16[768,2304]{1,0:T(8,128)(2,1)} async-done(((bf16[96,2304]{1,0:T(8,128)(2,1)}), bf16[768,2304]{1,0:T(8,128)(2,1)}) %all-gather.5.cloned.1.call-update) | async-done | bytes 3538960 | tf_op jit(solution)/shard_map/all_gather | solution.py:77
  78.4 6.2 fusion.63
  84.6 1.3 slice.141
  85.9 3.1 fusion.86
  89.0 3.6 copy.51
  92.5 1.7 copy.50
  94.3 3.5 copy.52
  97.8 2.4 slice_negate_fusion.2
  101.1 1.4 copy-done.6
  102.5 1.9 fusion.32
  104.4 10.9 %fusion.13 = (f32[12,512]{1,0:T(8,128)S(1)}, f32[12,512,1024]{2,1,0:T(8,128)}) fusion(pred[512,1024]{1,0:T(8,128)(4,1)S(1)} %copy-done.16, bf16[1024,12,64]{0,2,1:T(8,128)(2,1)S(1)} %get-tuple-element.73, bf16[1024,12,64]{0,2,1:T(8,128)(2,1)S(1)} %get-tuple-element.72), kind=kOutput, calls=%fused_computation.24 | convolution fusion | flops 824174592 | bytes 28073984 | tf_op jit(solution)/shard_map/qhd,khd->hqk/dot_general | solution.py:54
  115.4 10.7 %fusion.12 = (f32[12,512]{1,0:T(8,128)S(1)}, f32[12,512,1024]{2,1,0:T(8,128)}) fusion(pred[512,1024]{1,0:T(8,128)(4,1)S(1)} %copy-done.13, bf16[1024,12,64]{0,2,1:T(8,128)(2,1)S(1)} %get-tuple-element.73, bf16[1024,12,64]{0,2,1:T(8,128)(2,1)S(1)} %get-tuple-element.72), kind=kOutput, calls=%fused_computation.23 | convolution fusion | flops 824174592 | bytes 28073984 | tf_op jit(solution)/shard_map/qhd,khd->hqk/dot_general | solution.py:54
  126.1 12.1 %fusion.1 = f32[12,512]{1,0:T(8,128)S(1)} fusion(f32[12,512]{1,0:T(8,128)S(1)} %get-tuple-element.84, f32[12,512,1024]{2,1,0:T(8,128)} %get-tuple-element.85, pred[512,1024]{1,0:T(8,128)(4,1)S(1)} %copy-done.16), kind=kLoop, calls=%fused_computation.13 | loop fusion | flops 25159680 | bytes 25739264 | tf_op jit(solution)/shard_map/reduce_sum | solution.py:107
  138.2 13.8 %fusion.45 = bf16[12,64,512]{2,1,0:T(8,128)(2,1)} fusion(bf16[1024,12,64]{0,2,1:T(8,128)(2,1)S(1)} %bitcast.68, f32[12,512]{1,0:T(8,128)S(1)} %fusion.1, f32[12,512]{1,0:T(8,128)S(1)} %get-tuple-element.84, f32[12,512,1024]{2,1,0:T(8,128)} %get-tuple-element.85, pred[512,1024]{1,0:T(8,128)(4,1)S(1)} %copy-done.16), kind=kOutput, calls=%fused_computation.101 | convolution fusion | flops 837156864 | bytes 28098560 | tf_op jit(solution)/shard_map/hqk,khd->qhd/dot_general | solution.py:110
  153.0 1.4 slice-done.5
  154.4 7.3 fusion
  161.7 8.6 %fusion.46 = bf16[12,64,512]{2,1,0:T(8,128)(2,1)} fusion(bf16[1024,12,64]{0,2,1:T(8,128)(2,1)S(1)} %bitcast.69, f32[12,512]{1,0:T(8,128)S(1)} %fusion, f32[12,512]{1,0:T(8,128)S(1)} %get-tuple-element.86, f32[12,512,1024]{2,1,0:T(8,128)S(1)} %bitcast.61, pred[512,1024]{1,0:T(8,128)(4,1)S(1)} %copy-done.13), kind=kOutput, calls=%fused_computation.102 | convolution fusion | flops 837156864 | bytes 28098560 | tf_op jit(solution)/shard_map/hqk,khd->qhd/dot_general | solution.py:110
  170.3 3.3 fusion.92
  175.3 11.1 %all-gather.9.cloned.1.call-done = bf16[768,2304]{1,0:T(8,128)(2,1)} async-done(((bf16[96,2304]{1,0:T(8,128)(2,1)}), bf16[768,2304]{1,0:T(8,128)(2,1)}) %all-gather.9.cloned.1.call-update) | async-done | bytes 3538960 | tf_op jit(solution)/shard_map/all_gather | solution.py:79
  186.4 10.6 %fusion.83 = f32[1024,2304]{1,0:T(8,128)} fusion(bf16[768,2304]{1,0:T(8,128)(2,1)} %all-gather.9.cloned.1.call-done, f32[1024,768]{0,1:T(8,128)} %copy-done.19, f32[768]{0:T(1024)S(1)} %copy-done.53, f32[1024]{0:T(1024)S(1)} %fusion.68, f32[1024]{0:T(1024)S(1)} %broadcast_multiply_fusion.3), kind=kOutput, calls=%fused_computation.155 | convolution fusion | flops 3627024384 | bytes 16133120 | tf_op jit(solution)/shard_map/dot_general | solution.py:115
  197.0 35.9 %all-gather.11.cloned.1.call-done = bf16[768,1152]{1,0:T(8,128)(2,1)} async-done(((bf16[96,1152]{1,0:T(8,128)(2,1)}), bf16[768,1152]{1,0:T(8,128)(2,1)}) %all-gather.11.cloned.1.call-update) | async-done | bytes 1769488 | tf_op jit(solution)/shard_map/all_gather | solution.py:80
  232.9 15.2 %fusion.44 = (f32[1024,1152]{1,0:T(8,128)}, f32[1024,1152]{1,0:T(8,128)S(1)}, f32[1024,1152]{1,0:T(8,128)S(1)}) fusion(f32[1024,2304]{1,0:T(8,128)} %fusion.83, bf16[768,1152]{1,0:T(8,128)(2,1)} %all-gather.11.cloned.1.call-done, bf16[1024,768]{0,1:T(8,128)(2,1)S(1)} %copy-done.9, f32[1024]{0:T(1024)S(1)} %copy-done.42), kind=kOutput, calls=%fused_computation.98 | convolution fusion | flops 1890975744 | bytes 22220800 | tf_op jit(solution)/shard_map/dot_general | solution.py:133
  248.0 3.5 multiply_add_fusion
  251.6 9.5 %multiply_reduce_fusion.2 = (f32[768]{0:T(1024)}, f32[1024]{0:T(1024)S(1)}, f32[1024,768]{0,1:T(8,128)S(1)}) fusion(f32[1024,768]{0,1:T(8,128)S(1)} %copy-done.20, f32[1024]{0:T(1024)S(1)} %fusion.68, f32[1024]{0:T(1024)S(1)} %broadcast_multiply_fusion.3, f32[768]{0:T(1024)S(1)} %copy-done.53, bf16[768,2304]{1,0:T(8,128)(2,1)} %all-gather.9.cloned.1.call-done, ...), kind=kOutput, calls=%fused_computation.76 | convolution fusion | flops 3634100480 | bytes 19286016 | tf_op jit(solution)/shard_map/tf,df->td/dot_general | solution.py:137
  264.8 2.9 fusion.51
  267.7 5.7 fusion.47
  273.5 3.3 convolution_convert_fusion
  279.3 9.1 %fusion.59 = f32[768,2304]{1,0:T(8,128)} fusion(f32[1024,1152]{1,0:T(8,128)S(1)} %bitcast.77, f32[1024,1152]{1,0:T(8,128)} %get-tuple-element.56, f32[1024,768]{0,1:T(8,128)S(1)} %copy-done.21, f32[768]{0:T(1024)S(1)} %copy-done.53, f32[1024]{0:T(1024)S(1)} %fusion.68, f32[1024]{0:T(1024)S(1)} %broadcast_multiply_fusion.3), kind=kOutput, calls=%fused_computation.113 | convolution fusion | flops 3631742976 | bytes 19672064 | tf_op jit(solution)/shard_map/td,tf->df/dot_general | solution.py:136
  289.5 18.0 %multiply_reduce_fusion.1 = (f32[12,512]{1,0:T(8,128)S(1)}, f32[12,512,1024]{2,1,0:T(8,128)}) fusion(f32[12,512]{1,0:T(8,128)S(1)} %log_add_fusion.1, f32[12,512,1024]{2,1,0:T(8,128)} %get-tuple-element.87, pred[512,1024]{1,0:T(8,128)(4,1)S(1)} %copy-done.14, bf16[512,12,64]{0,2,1:T(8,128)(2,1)} %bitcast.78, bf16[1024,12,64]{0,2,1:T(8,128)(2,1)S(1)} %bitcast.70), kind=kOutput, calls=%fused_computation.4 | convolution fusion | flops 836757504 | bytes 53264384 | tf_op jit(solution)/shard_map/qhd,khd->hqk/dot_general | solution.py:164
  307.5 17.8 %multiply_reduce_fusion = (f32[12,512]{1,0:T(8,128)S(1)}, f32[12,512,1024]{2,1,0:T(8,128)}) fusion(f32[12,512]{1,0:T(8,128)S(1)} %log_add_fusion, f32[12,512,1024]{2,1,0:T(8,128)} %get-tuple-element.85, pred[512,1024]{1,0:T(8,128)(4,1)S(1)} %copy-done.17, bf16[512,12,64]{0,2,1:T(8,128)(2,1)} %bitcast.80, bf16[1024,12,64]{0,2,1:T(8,128)(2,1)S(1)} %bitcast.71), kind=kOutput, calls=%fused_computation.1 | convolution fusion | flops 836757504 | bytes 53264384 | tf_op jit(solution)/shard_map/qhd,khd->hqk/dot_general | solution.py:164
  325.4 42.7 %multiply_convert_fusion = (bf16[12,512,1024]{2,1,0:T(8,128)(2,1)}, bf16[12,512,1024]{2,1,0:T(8,128)(2,1)}) fusion(f32[12,512,1024]{2,1,0:T(8,128)} %get-tuple-element.95, f32[12,512]{1,0:T(8,128)S(1)} %get-tuple-element.94, f32[12,512]{1,0:T(8,128)S(1)} %log_add_fusion, f32[12,512,1024]{2,1,0:T(8,128)} %get-tuple-element.85, ...), kind=kLoop, calls=%fused_computation | loop fusion | flops 75497472 | bytes 126976000 | tf_op jit(solution)/shard_map/convert_element_type | solution.py:168
  368.1 10.4 %convolution_multiply_fusion = f32[12,64,512]{2,1,0:T(8,128)} fusion(bf16[1024,12,64]{0,2,1:T(8,128)(2,1)} %copy-done.3, bf16[12,512,1024]{2,1,0:T(8,128)(2,1)} %get-tuple-element.100), kind=kOutput, calls=%fused_computation.99 | convolution fusion | flops 805699584 | bytes 15728640 | tf_op jit(solution)/shard_map/hqk,khd->qhd/dot_general | solution.py:170
  378.5 6.6 convolution_multiply_fusion.1
  385.1 2.3 maximum_multiply_fusion.3
  389.6 2.1 fusion.36
  391.7 2.3 fusion.55
  395.5 3.7 bitcast_multiply_fusion
  401.6 12.1 %fusion.4 = f32[12,64,1024]{2,1,0:T(8,128)S(1)} fusion(bf16[512,12,64]{0,2,1:T(8,128)(2,1)S(1)} %bitcast.81, f32[12,512]{1,0:T(8,128)S(1)} %log_add_fusion, f32[12,512,1024]{2,1,0:T(8,128)} %get-tuple-element.85, pred[512,1024]{1,0:T(8,128)(4,1)S(1)} %copy-done.18), kind=kOutput, calls=%fused_computation.16 | convolution fusion | flops 830472192 | bytes 29646848 | tf_op jit(solution)/shard_map/hqk,qhd->khd/dot_general | solution.py:161
  413.7 12.0 %add_convert_fusion.1 = bf16[12,64,1024]{2,1,0:T(8,128)(2,1)S(1)} fusion(f32[12,64,1024]{2,1,0:T(8,128)S(1)} %fusion.4, bf16[512,12,64]{0,2,1:T(8,128)(2,1)S(1)} %bitcast.79, f32[12,512]{1,0:T(8,128)S(1)} %log_add_fusion.1, f32[12,512,1024]{2,1,0:T(8,128)} %get-tuple-element.87, pred[512,1024]{1,0:T(8,128)(4,1)S(1)} %copy-done.15), kind=kOutput, calls=%fused_computation.78 | convolution fusion | flops 832045056 | bytes 31219712 | tf_op jit(solution)/shard_map/hqk,qhd->khd/dot_general | solution.py:161
  426.9 6.8 fusion.39
  434.4 7.0 fusion.30
  441.5 1.6 copy-done.23
  443.1 1.3 fusion.28
  444.5 3.4 add_convert_fusion.2
  447.9 1.6 convert_element_type.166
  449.5 1.7 convert_element_type.170
  451.2 98.6 %reduce-scatter.9.cloned.1.call-done = f32[96,2304]{1,0:T(8,128)} async-done(((f32[768,2304]{1,0:T(8,128)}), f32[96,2304]{1,0:T(8,128)}) %reduce-scatter.9.cloned.1.call-update) | async-done | bytes 884752 | tf_op jit(solution)/shard_map/reduce_scatter | solution.py:199
  549.8 2.0 convert_element_type.168
  551.8 130.2 %reduce-scatter.5.cloned.1.call-done = f32[96,2304]{1,0:T(8,128)} async-done(((f32[768,2304]{1,0:T(8,128)}), f32[96,2304]{1,0:T(8,128)}) %reduce-scatter.5.cloned.1.call-update) | async-done | bytes 884752 | tf_op jit(solution)/shard_map/reduce_scatter | solution.py:197
  682.0 2.0 convert_element_type.164
  684.0 2.6 copy.55
  686.6 19.7 %all-reduce.6 = (bf16[768]{0:T(1024)(128)(2,1)S(1)}, bf16[768]{0:T(1024)(128)(2,1)S(1)}) all-reduce(f32[768]{0:T(1024)S(1)} %get-tuple-element.42, f32[768]{0:T(1024)S(1)} %copy-done.54), channel_id=6, replica_groups=mesh['fsdp'=8,'rep'=4] {'fsdp'}, use_global_device_ids=true, to_apply=%region_24.25.clone | all-reduce | flops 1536 | bytes 9216
  706.5 5.6 all-reduce.8
  713.1 6.1 add_add_fusion.2
  719.2 3.6 copy.56
  723.3 1.6 convert_element_type.167
  724.9 2.0 convert_element_type.165
  726.9 1.7 convert_element_type.171
  728.7 2.0 convert_element_type.169
  (202 shorter events, 32.0 us)
Async XLA Ops:
  7.2 36.7 %copy-start.34 = (bf16[1024,768]{1,0:T(8,128)(2,1)S(1)}, bf16[1024,768]{1,0:T(8,128)(2,1)}, u32[]{:S(2)}) copy-start(bf16[1024,768]{1,0:T(8,128)(2,1)} %param.10) | copy-start | bytes 4718596
  7.2 71.2 %all-gather.5.cloned.1.call-start = ((), (), s32[]{:S(2)}) async-start(), calls=%async_computation.4 | async-start | bytes 3981312 | tf_op jit(solution)/shard_map/all_gather | solution.py:77
  7.9 162.4 %all-gather.7.cloned.1.call-start = ((), (), s32[]{:S(2)}) async-start(), calls=%async_computation.5 | async-start | bytes 1327104 | tf_op jit(solution)/shard_map/all_gather | solution.py:78
  8.7 177.7 %all-gather.9.cloned.1.call-start = ((), (), s32[]{:S(2)}) async-start(), calls=%async_computation.6 | async-start | bytes 3981312 | tf_op jit(solution)/shard_map/all_gather | solution.py:79
  9.4 223.5 %all-gather.11.cloned.1.call-start = ((), (), s32[]{:S(2)}) async-start(), calls=%async_computation.7 | async-start | bytes 1990656 | tf_op jit(solution)/shard_map/all_gather | solution.py:80
  10.0 437.9 %reduce-scatter.7.cloned.1.call-start = ((), (), s32[]{:S(2)}) async-start(), calls=%async_computation.9 | async-start | bytes 2654208 | tf_op jit(solution)/shard_map/reduce_scatter | solution.py:198
  40.7 37.7 %copy-start.44 = (f32[768]{0:T(1024)}, f32[768]{0:T(1024)S(1)}, u32[]{:S(2)}) copy-start(f32[768]{0:T(1024)S(1)} %convert_element_type.135) | copy-start | bytes 9220
  43.9 57.2 %copy-start.29 = (f32[1024,64]{0,1:T(8,128)}, f32[1024,64]{0,1:T(8,128)S(1)}, u32[]{:S(2)}) copy-start(f32[1024,64]{0,1:T(8,128)S(1)} %get-tuple-element.77) | copy-start | bytes 786436
  44.7 125.7 %copy-start.1 = (bf16[1024,768]{0,1:T(8,128)(2,1)}, bf16[1024,768]{0,1:T(8,128)(2,1)S(1)}, u32[]{:S(2)}) copy-start(bf16[1024,768]{0,1:T(8,128)(2,1)S(1)} %copy.49) | copy-start | bytes 4718596
  44.7 2.0 copy-start.35
  44.7 3.6 copy-start.52
  45.0 39.6 %copy-start.40 = (f32[1024]{0:T(1024)}, f32[1024]{0:T(1024)S(1)}, u32[]{:S(2)}) copy-start(f32[1024]{0:T(1024)S(1)} %broadcast_multiply_fusion.4) | copy-start | bytes 12292
  46.6 38.0 %copy-start.46 = (f32[1024]{0:T(1024)}, f32[1024]{0:T(1024)S(1)}, u32[]{:S(2)}) copy-start(f32[1024]{0:T(1024)S(1)} %fusion.67) | copy-start | bytes 12292
  97.8 2.8 copy-start.5
  100.6 1.9 copy-start.6
  100.6 1.9 copy-start.31
  104.4 11.0 %copy-start.3 = (bf16[1024,12,64]{0,2,1:T(8,128)(2,1)}, bf16[1024,12,64]{0,2,1:T(8,128)(2,1)S(1)}, u32[]{:S(2)}) copy-start(bf16[1024,12,64]{0,2,1:T(8,128)(2,1)S(1)} %get-tuple-element.73) | copy-start | bytes 4718596
  104.4 11.0 %copy-start.7 = (bf16[1024,12,64]{0,2,1:T(8,128)(2,1)}, bf16[1024,12,64]{0,2,1:T(8,128)(2,1)S(1)}, u32[]{:S(2)}) copy-start(bf16[1024,12,64]{0,2,1:T(8,128)(2,1)S(1)} %get-tuple-element.72) | copy-start | bytes 4718596
  104.4 10.9 %copy-start.13 = (pred[512,1024]{1,0:T(8,128)(4,1)S(1)}, pred[512,1024]{1,0:T(8,128)(4,1)}, u32[]{:S(2)}) copy-start(pred[512,1024]{1,0:T(8,128)(4,1)} %get-tuple-element.78) | copy-start | bytes 1572868
  138.2 13.9 %slice-start = ((s8[25165824]{0:T(1024)(128)(4,1)}), s8[4194304]{0:T(1024)(128)(4,1)S(1)}, s32[]{:S(2)}) async-start(s8[25165824]{0:T(1024)(128)(4,1)} %bitcast.60), calls=%async_computation.13 | async-start | bytes 8388608
  138.2 13.8 %slice-start.1 = ((s8[25165824]{0:T(1024)(128)(4,1)}), s8[4194304]{0:T(1024)(128)(4,1)S(1)}, s32[]{:S(2)}) async-start(s8[25165824]{0:T(1024)(128)(4,1)} %bitcast.60), calls=%async_computation.14 | async-start | bytes 8388608
  138.2 13.8 %slice-start.2 = ((s8[25165824]{0:T(1024)(128)(4,1)}), s8[4194304]{0:T(1024)(128)(4,1)S(1)}, s32[]{:S(2)}) async-start(s8[25165824]{0:T(1024)(128)(4,1)} %bitcast.60), calls=%async_computation.15 | async-start | bytes 8388608
  138.2 13.8 %slice-start.3 = ((s8[25165824]{0:T(1024)(128)(4,1)}), s8[4194304]{0:T(1024)(128)(4,1)S(1)}, s32[]{:S(2)}) async-start(s8[25165824]{0:T(1024)(128)(4,1)} %bitcast.60), calls=%async_computation.16 | async-start | bytes 8388608
  138.2 14.8 %slice-start.4 = ((s8[25165824]{0:T(1024)(128)(4,1)}), s8[4194304]{0:T(1024)(128)(4,1)S(1)}, s32[]{:S(2)}) async-start(s8[25165824]{0:T(1024)(128)(4,1)} %bitcast.60), calls=%async_computation.17 | async-start | bytes 8388608
  138.2 16.1 %slice-start.5 = ((s8[25165824]{0:T(1024)(128)(4,1)}), s8[4194304]{0:T(1024)(128)(4,1)S(1)}, s32[]{:S(2)}) async-start(s8[25165824]{0:T(1024)(128)(4,1)} %bitcast.60), calls=%async_computation.18 | async-start | bytes 8388608
  173.6 12.7 %copy-start.53 = (f32[768]{0:T(1024)S(1)}, f32[768]{0:T(1024)}, u32[]{:S(2)}) copy-start(f32[768]{0:T(1024)} %convert_element_type.150) | copy-start | bytes 9220
  175.3 57.6 %copy-start.9 = (bf16[1024,768]{0,1:T(8,128)(2,1)S(1)}, bf16[1024,768]{0,1:T(8,128)(2,1)}, u32[]{:S(2)}) copy-start(bf16[1024,768]{0,1:T(8,128)(2,1)} %copy.54) | copy-start | bytes 4718596
  175.3 57.6 %copy-start.42 = (f32[1024]{0:T(1024)S(1)}, f32[1024]{0:T(1024)}, u32[]{:S(2)}) copy-start(f32[1024]{0:T(1024)} %convert_element_type.155) | copy-start | bytes 12292
  232.9 15.2 %copy-start.24 = (f32[1024,2304]{1,0:T(8,128)S(1)}, f32[1024,2304]{1,0:T(8,128)}, u32[]{:S(2)}) copy-start(f32[1024,2304]{1,0:T(8,128)} %fusion.83) | copy-start | bytes 28311556
  248.0 3.5 copy-start.20
  251.6 9.6 %copy-start.25 = (f32[1024,1152]{1,0:T(8,128)}, f32[1024,1152]{1,0:T(8,128)S(1)}, u32[]{:S(2)}) copy-start(f32[1024,1152]{1,0:T(8,128)S(1)} %get-tuple-element.58) | copy-start | bytes 14155780
  261.9 2.8 copy-start.57
  262.0 2.8 copy-start.58
  267.7 181.8 %reduce-scatter.11.cloned.1.call-start = ((), (), s32[]{:S(2)}) async-start(), calls=%async_computation.11 | async-start | bytes 3981312 | tf_op jit(solution)/shard_map/reduce_scatter | solution.py:200
  273.4 4.7 slice-start.9
  273.4 276.4 %reduce-scatter.9.cloned.1.call-start = ((), (), s32[]{:S(2)}) async-start(), calls=%async_computation.10 | async-start | bytes 7962624 | tf_op jit(solution)/shard_map/reduce_scatter | solution.py:199
  273.5 4.6 slice-start.10
  276.9 2.5 copy-start.21
  288.5 393.5 %reduce-scatter.5.cloned.1.call-start = ((), (), s32[]{:S(2)}) async-start(), calls=%async_computation.8 | async-start | bytes 7962624 | tf_op jit(solution)/shard_map/reduce_scatter | solution.py:197
  289.5 18.0 %copy-start.17 = (pred[512,1024]{1,0:T(8,128)(4,1)S(1)}, pred[512,1024]{1,0:T(8,128)(4,1)}, u32[]{:S(2)}) copy-start(pred[512,1024]{1,0:T(8,128)(4,1)} %get-tuple-element.79) | copy-start | bytes 1572868
  368.0 10.4 %copy-start = (bf16[12,512,1024]{2,1,0:T(8,128)(2,1)S(1)}, bf16[12,512,1024]{2,1,0:T(8,128)(2,1)}, u32[]{:S(2)}) copy-start(bf16[12,512,1024]{2,1,0:T(8,128)(2,1)} %get-tuple-element.101) | copy-start | bytes 37748740
  378.5 6.6 copy-start.32
  389.6 2.1 copy-start.8
  389.6 4.4 slice-start.6
  391.7 2.7 slice-start.7
  391.7 3.9 slice-start.8
  391.7 3.9 copy-start.28
  401.6 24.1 %copy-start.38 = (bf16[1024,12,64]{0,2,1:T(8,128)(2,1)}, bf16[1024,12,64]{0,2,1:T(8,128)(2,1)S(1)}, u32[]{:S(2)}) copy-start(bf16[1024,12,64]{0,2,1:T(8,128)(2,1)S(1)} %fusion.37) | copy-start | bytes 4718596
  401.6 12.1 %copy-start.15 = (pred[512,1024]{1,0:T(8,128)(4,1)S(1)}, pred[512,1024]{1,0:T(8,128)(4,1)}, u32[]{:S(2)}) copy-start(pred[512,1024]{1,0:T(8,128)(4,1)} %get-tuple-element.78) | copy-start | bytes 1572868
  401.6 12.1 %copy-start.26 = (bf16[512,768]{0,1:T(8,128)(2,1)S(1)}, bf16[512,768]{0,1:T(8,128)(2,1)}, u32[]{:S(2)}) copy-start(bf16[512,768]{0,1:T(8,128)(2,1)} %get-tuple-element.70) | copy-start | bytes 2359300
  413.7 13.2 %copy-start.2 = (bf16[1024,768]{0,1:T(8,128)(2,1)S(1)}, bf16[1024,768]{0,1:T(8,128)(2,1)}, u32[]{:S(2)}) copy-start(bf16[1024,768]{0,1:T(8,128)(2,1)} %copy-done.1) | copy-start | bytes 4718596
  413.7 13.2 %copy-start.37 = (bf16[1024,768]{0,1:T(8,128)(2,1)S(1)}, bf16[1024,768]{0,1:T(8,128)(2,1)}, u32[]{:S(2)}) copy-start(bf16[1024,768]{0,1:T(8,128)(2,1)} %fusion.36) | copy-start | bytes 4718596
  413.7 13.2 %copy-start.41 = (f32[1024]{0:T(1024)S(1)}, f32[1024]{0:T(1024)}, u32[]{:S(2)}) copy-start(f32[1024]{0:T(1024)} %copy-done.40) | copy-start | bytes 12292
  413.7 13.2 %copy-start.45 = (f32[768]{0:T(1024)S(1)}, f32[768]{0:T(1024)}, u32[]{:S(2)}) copy-start(f32[768]{0:T(1024)} %copy-done.44) | copy-start | bytes 9220
  413.7 13.1 %copy-start.47 = (f32[1024]{0:T(1024)S(1)}, f32[1024]{0:T(1024)}, u32[]{:S(2)}) copy-start(f32[1024]{0:T(1024)} %copy-done.46) | copy-start | bytes 12292
  433.7 289.6 %all-reduce.12.cloned.1.call-start = ((), (), s32[]{:S(2)}) async-start(), calls=%async_computation.12 | async-start | bytes 2506752 | tf_op jit(solution)/shard_map/psum | solution.py:205
  434.4 7.1 copy-start.51
  434.4 10.0 %copy-start.33 = (bf16[1024,1152]{1,0:T(8,128)(2,1)S(1)}, bf16[1024,1152]{1,0:T(8,128)(2,1)}, u32[]{:S(2)}) copy-start(bf16[1024,1152]{1,0:T(8,128)(2,1)} %get-tuple-element.59) | copy-start | bytes 7077892
  434.4 10.0 %copy-start.55 = (bf16[768,1152]{1,0:T(8,128)(2,1)S(1)}, bf16[768,1152]{1,0:T(8,128)(2,1)}, u32[]{:S(2)}) copy-start(bf16[768,1152]{1,0:T(8,128)(2,1)} %all-gather.11.cloned.1.call-done) | copy-start | bytes 5308420
  441.4 3.0 copy-start.22
  551.8 134.8 %copy-start.54 = (f32[768]{0:T(1024)S(1)}, f32[768]{0:T(1024)}, u32[]{:S(2)}) copy-start(f32[768]{0:T(1024)} %get-tuple-element.40) | copy-start | bytes 9220
  551.8 161.3 %copy-start.10 = (bf16[1024,768]{0,1:T(8,128)(2,1)S(1)}, bf16[1024,768]{0,1:T(8,128)(2,1)}, u32[]{:S(2)}) copy-start(bf16[1024,768]{0,1:T(8,128)(2,1)} %copy.54) | copy-start | bytes 4718596
  551.8 161.3 %copy-start.43 = (f32[1024]{0:T(1024)S(1)}, f32[1024]{0:T(1024)}, u32[]{:S(2)}) copy-start(f32[1024]{0:T(1024)} %convert_element_type.155) | copy-start | bytes 12292
  551.8 161.3 %copy-start.49 = (f32[1024]{0:T(1024)S(1)}, f32[1024]{0:T(1024)}, u32[]{:S(2)}) copy-start(f32[1024]{0:T(1024)} %copy-done.48) | copy-start | bytes 12292
  (15 other events, 21.3 us)
Sparse Core Ops, SparseCore 0:
  10.2 68.1 all-gather.4
  80.6 39.5 all-gather.6
  122.4 63.9 all-gather.8
  188.4 44.4 all-gather.10
  267.8 67.9 reduce-scatter.6
  339.3 78.1 reduce-scatter.10
  421.2 128.5 reduce-scatter.8
  553.9 128.0 reduce-scatter.4
  685.2 38.0 all-reduce.11
where the time goes:
time: 747 us; the launch traced here: 737 us
  waiting for transfers between devices  307 us (41%)
  matrix products  210 us (28%)
  other arithmetic  109 us (15%)
  blocking collectives  48.8 us (7%)
  local copies, waits for them, and re-layouts  45.4 us (6%)
  between operations  16.1 us (2%)
    reduce_scatter x1, waiting for transfers between devices, on_device(): lax.psum_scatter(qkv_term, 'fsdp', scatter_dimension=0, tiled=True)  130 us
    reduce_scatter x1, waiting for transfers between devices, on_device(): lax.psum_scatter(wide_term, 'fsdp', scatter_dimension=0, tiled=True)  98.6 us
    unnamed x2, blocking collectives  43.2 us
    convert_element_type x1, other arithmetic, on_device(): grad_scores = (probs_f32 * (grad_probs - row_delta)).astype(jnp.bfloat16)  42.7 us
    all_gather x1, waiting for transfers between devices, on_device(): lax.all_gather(narrow_weight, 'fsdp', axis=0, tiled=True)  35.9 us
    dot_general x2, matrix products, on_device(): jnp.einsum('qhd,khd->hqk', grad_rows, valueset, preferred_element_type=jn...  35.9 us
    unnamed x151, local copies, waits for them, and re-layouts  29.4 us
    all_gather x1, waiting for transfers between devices, on_device(): lax.all_gather(qkv_weight, 'fsdp', axis=0, tiled=True)  28.4 us
  transfers between devices with their start and end apart: 9, of which 6 were waited for; matrix products, arithmetic and copies ran while one was open for 41% of the time, Pallas kernels for 0%

commit v1 on v0

--- a/solution.py
+++ b/solution.py
@@ -10,6 +10,19 @@
 rope_base = 160000.0
 eps = 1e-05
 masked_score = -1e30
+
+
+def gather_around(shard, axis, dim):
+    size, place, rows = (lax.axis_size(axis), lax.axis_index(axis), shard.shape[dim])
+    right = [(i, (i + 1) % size) for i in range(size)]
+    out = jnp.zeros((*shard.shape[:dim], size * rows, *shard.shape[dim + 1 :]), shard.dtype)
+    held = shard
+    for step in range(size):
+        owner = (place - step) % size
+        out = lax.dynamic_update_slice_in_dim(out, held, owner * rows, axis=dim)
+        if step < size - 1:
+            held = lax.ppermute(held, axis, right)
+    return out
 
 
 def layer_norm(values, scales):
@@ -77,7 +90,7 @@
         lax.all_gather(qkv_weight, "fsdp", axis=0, tiled=True),
         lax.all_gather(attn_weight, "fsdp", axis=0, tiled=True),
         lax.all_gather(wide_weight, "fsdp", axis=0, tiled=True),
-        lax.all_gather(narrow_weight, "fsdp", axis=0, tiled=True),
+        gather_around(narrow_weight, "fsdp", 0),
         lax.all_gather(first_gain, "fsdp", axis=0, tiled=True),
         lax.all_gather(second_gain, "fsdp", axis=0, tiled=True),
     )

time: 747 us -> 780 us (1.044)
  waiting for transfers between devices: 307 us -> 339 us
    ppermute x0 -> x7, waiting for transfers between devices: none -> 93.6 us  [gather_around(): held = lax.ppermute(held, axis, right)]
    reduce_scatter x1, waiting for transfers between devices: 98.6 us -> 36.6 us  [on_device(): lax.psum_scatter(wide_term, 'fsdp', scatter_dimension=0, tiled=True)]
    unnamed x151 -> x155, local copies, waits for them, and re-layouts: 29.4 us -> 30.4 us
  transfers between devices with their start and end apart: 9 -> 16, of which waited for: 6 -> 13; matrix products, arithmetic and copies ran while one was open for 41% -> 40% of each run, Pallas kernels for 0% -> 0%
where the time goes in v1:
time: 780 us; the launch traced here: 771 us
  waiting for transfers between devices  339 us (43%)
  matrix products  208 us (27%)
  other arithmetic  109 us (14%)
  blocking collectives  48.8 us (6%)
  local copies, waits for them, and re-layouts  47.7 us (6%)
  between operations  16.1 us (2%)
    reduce_scatter x1, waiting for transfers between devices, on_device(): lax.psum_scatter(qkv_term, 'fsdp', scatter_dimension=0, tiled=True)  130 us
    ppermute x7, waiting for transfers between devices, gather_around(): held = lax.ppermute(held, axis, right)  93.6 us
    unnamed x2, blocking collectives  43.2 us
    convert_element_type x1, other arithmetic, on_device(): grad_scores = (probs_f32 * (grad_probs - row_delta)).astype(jnp.bfloat16)  42.6 us
    reduce_scatter x1, waiting for transfers between devices, on_device(): lax.psum_scatter(wide_term, 'fsdp', scatter_dimension=0, tiled=True)  36.6 us
    all_gather x1, waiting for transfers between devices, on_device(): lax.all_gather(narrow_weight, 'fsdp', axis=0, tiled=True)  35.8 us
    dot_general x2, matrix products, on_device(): jnp.einsum('qhd,khd->hqk', grad_rows, valueset, preferred_element_type=jn...  35.8 us
    unnamed x155, local copies, waits for them, and re-layouts  30.4 us
  transfers between devices with their start and end apart: 16, of which 13 were waited for; matrix products, arithmetic and copies ran while one was open for 40% of the time, Pallas kernels for 0%

profile of v1, /device:TPU:0, one launch (start us, length us, event | category | flops | bytes accessed | tf_op | source)
XLA Modules:
  0.0 770.5 jit_solution(3531391745146600196)
XLA Ops:
  17.2 23.5 %all-reduce.7 = (bf16[768]{0:T(1024)(128)(2,1)S(1)}, bf16[768]{0:T(1024)(128)(2,1)S(1)}) all-reduce(bf16[768]{0:T(1024)(128)(2,1)S(1)} %dynamic-update-slice, bf16[768]{0:T(1024)(128)(2,1)S(1)} %dynamic-update-slice.1), channel_id=1, replica_groups=mesh['fsdp'=8,'rep'=4] {'fsdp'}, use_global_device_ids=true, to_apply=%add.2 | all-reduce | flops 1536 | bytes 6144
  42.2 1.7 broadcast_multiply_fusion.1
  48.3 1.7 compare_and_fusion.1
  50.0 28.4 %all-gather.5.cloned.1.call-done = bf16[768,2304]{1,0:T(8,128)(2,1)} async-done(((bf16[96,2304]{1,0:T(8,128)(2,1)}), bf16[768,2304]{1,0:T(8,128)(2,1)}) %all-gather.5.cloned.1.call-update) | async-done | bytes 3538960 | tf_op jit(solution)/shard_map/all_gather | solution.py:90
  78.4 6.2 fusion.63
  85.9 3.1 fusion.86
  89.0 3.6 copy.51
  92.5 1.7 copy.50
  94.3 3.5 copy.52
  97.8 2.4 slice_negate_fusion.2
  102.5 1.9 fusion.32
  104.4 10.8 %fusion.13 = (f32[12,512]{1,0:T(8,128)S(1)}, f32[12,512,1024]{2,1,0:T(8,128)}) fusion(pred[512,1024]{1,0:T(8,128)(4,1)S(1)} %copy-done.16, bf16[1024,12,64]{0,2,1:T(8,128)(2,1)S(1)} %get-tuple-element.73, bf16[1024,12,64]{0,2,1:T(8,128)(2,1)S(1)} %get-tuple-element.72), kind=kOutput, calls=%fused_computation.24 | convolution fusion | flops 824174592 | bytes 28073984 | tf_op jit(solution)/shard_map/qhd,khd->hqk/dot_general | solution.py:67
  115.3 10.7 %fusion.12 = (f32[12,512]{1,0:T(8,128)S(1)}, f32[12,512,1024]{2,1,0:T(8,128)}) fusion(pred[512,1024]{1,0:T(8,128)(4,1)S(1)} %copy-done.13, bf16[1024,12,64]{0,2,1:T(8,128)(2,1)S(1)} %get-tuple-element.73, bf16[1024,12,64]{0,2,1:T(8,128)(2,1)S(1)} %get-tuple-element.72), kind=kOutput, calls=%fused_computation.23 | convolution fusion | flops 824174592 | bytes 28073984 | tf_op jit(solution)/shard_map/qhd,khd->hqk/dot_general | solution.py:67
  126.0 12.0 %fusion.1 = f32[12,512]{1,0:T(8,128)S(1)} fusion(f32[12,512]{1,0:T(8,128)S(1)} %get-tuple-element.84, f32[12,512,1024]{2,1,0:T(8,128)} %get-tuple-element.85, pred[512,1024]{1,0:T(8,128)(4,1)S(1)} %copy-done.16), kind=kLoop, calls=%fused_computation.13 | loop fusion | flops 25159680 | bytes 25739264 | tf_op jit(solution)/shard_map/reduce_sum | solution.py:120
  138.1 13.8 %fusion.45 = bf16[12,64,512]{2,1,0:T(8,128)(2,1)} fusion(bf16[1024,12,64]{0,2,1:T(8,128)(2,1)S(1)} %bitcast.68, f32[12,512]{1,0:T(8,128)S(1)} %fusion.1, f32[12,512]{1,0:T(8,128)S(1)} %get-tuple-element.84, f32[12,512,1024]{2,1,0:T(8,128)} %get-tuple-element.85, pred[512,1024]{1,0:T(8,128)(4,1)S(1)} %copy-done.16), kind=kOutput, calls=%fused_computation.101 | convolution fusion | flops 837156864 | bytes 28098560 | tf_op jit(solution)/shard_map/hqk,khd->qhd/dot_general | solution.py:123
  154.2 7.3 fusion
  161.5 8.7 %fusion.46 = bf16[12,64,512]{2,1,0:T(8,128)(2,1)} fusion(bf16[1024,12,64]{0,2,1:T(8,128)(2,1)S(1)} %bitcast.69, f32[12,512]{1,0:T(8,128)S(1)} %fusion, f32[12,512]{1,0:T(8,128)S(1)} %get-tuple-element.86, f32[12,512,1024]{2,1,0:T(8,128)S(1)} %bitcast.61, pred[512,1024]{1,0:T(8,128)(4,1)S(1)} %copy-done.13), kind=kOutput, calls=%fused_computation.102 | convolution fusion | flops 837156864 | bytes 28098560 | tf_op jit(solution)/shard_map/hqk,khd->qhd/dot_general | solution.py:123
  170.2 3.3 fusion.92
  175.2 11.2 %all-gather.9.cloned.1.call-done = bf16[768,2304]{1,0:T(8,128)(2,1)} async-done(((bf16[96,2304]{1,0:T(8,128)(2,1)}), bf16[768,2304]{1,0:T(8,128)(2,1)}) %all-gather.9.cloned.1.call-update) | async-done | bytes 3538960 | tf_op jit(solution)/shard_map/all_gather | solution.py:92
  186.4 10.6 %fusion.83 = f32[1024,2304]{1,0:T(8,128)} fusion(bf16[768,2304]{1,0:T(8,128)(2,1)} %all-gather.9.cloned.1.call-done, f32[1024,768]{0,1:T(8,128)} %copy-done.19, f32[768]{0:T(1024)S(1)} %copy-done.55, f32[1024]{0:T(1024)S(1)} %fusion.68, f32[1024]{0:T(1024)S(1)} %broadcast_multiply_fusion.3), kind=kOutput, calls=%fused_computation.163 | convolution fusion | flops 3627024384 | bytes 16133120 | tf_op jit(solution)/shard_map/dot_general | solution.py:128
  197.0 35.8 %all-gather.11.cloned.1.call-done = bf16[768,1152]{1,0:T(8,128)(2,1)} async-done(((bf16[96,1152]{1,0:T(8,128)(2,1)}), bf16[768,1152]{1,0:T(8,128)(2,1)}) %all-gather.11.cloned.1.call-update) | async-done | bytes 1769488 | tf_op jit(solution)/shard_map/all_gather | solution.py:137
  232.9 15.2 %fusion.44 = (f32[1024,1152]{1,0:T(8,128)}, f32[1024,1152]{1,0:T(8,128)S(1)}, f32[1024,1152]{1,0:T(8,128)S(1)}) fusion(f32[1024,2304]{1,0:T(8,128)} %fusion.83, bf16[768,1152]{1,0:T(8,128)(2,1)} %all-gather.11.cloned.1.call-done, bf16[1024,768]{0,1:T(8,128)(2,1)S(1)} %copy-done.9, f32[1024]{0:T(1024)S(1)} %copy-done.44), kind=kOutput, calls=%fused_computation.98 | convolution fusion | flops 1890975744 | bytes 22220800 | tf_op jit(solution)/shard_map/dot_general | solution.py:146
  248.0 3.5 multiply_add_fusion
  251.5 9.6 %multiply_reduce_fusion.2 = (f32[768]{0:T(1024)}, f32[1024]{0:T(1024)S(1)}, f32[1024,768]{0,1:T(8,128)S(1)}) fusion(f32[1024,768]{0,1:T(8,128)S(1)} %copy-done.20, f32[1024]{0:T(1024)S(1)} %fusion.68, f32[1024]{0:T(1024)S(1)} %broadcast_multiply_fusion.3, f32[768]{0:T(1024)S(1)} %copy-done.55, bf16[768,2304]{1,0:T(8,128)(2,1)} %all-gather.9.cloned.1.call-done, ...), kind=kOutput, calls=%fused_computation.76 | convolution fusion | flops 3634100480 | bytes 19286016 | tf_op jit(solution)/shard_map/tf,df->td/dot_general | solution.py:150
  264.8 2.9 fusion.51
  267.7 5.7 fusion.47
  273.5 3.3 convolution_convert_fusion
  279.3 9.1 %fusion.59 = f32[768,2304]{1,0:T(8,128)} fusion(f32[1024,1152]{1,0:T(8,128)S(1)} %bitcast.77, f32[1024,1152]{1,0:T(8,128)} %get-tuple-element.56, f32[1024,768]{0,1:T(8,128)S(1)} %copy-done.21, f32[768]{0:T(1024)S(1)} %copy-done.55, f32[1024]{0:T(1024)S(1)} %fusion.68, f32[1024]{0:T(1024)S(1)} %broadcast_multiply_fusion.3), kind=kOutput, calls=%fused_computation.113 | convolution fusion | flops 3631742976 | bytes 19672064 | tf_op jit(solution)/shard_map/td,tf->df/dot_general | solution.py:149
  289.5 18.0 %multiply_reduce_fusion.1 = (f32[12,512]{1,0:T(8,128)S(1)}, f32[12,512,1024]{2,1,0:T(8,128)}) fusion(f32[12,512]{1,0:T(8,128)S(1)} %log_add_fusion.1, f32[12,512,1024]{2,1,0:T(8,128)} %get-tuple-element.87, pred[512,1024]{1,0:T(8,128)(4,1)S(1)} %copy-done.14, bf16[512,12,64]{0,2,1:T(8,128)(2,1)} %bitcast.78, bf16[1024,12,64]{0,2,1:T(8,128)(2,1)S(1)} %bitcast.70), kind=kOutput, calls=%fused_computation.4 | convolution fusion | flops 836757504 | bytes 53264384 | tf_op jit(solution)/shard_map/qhd,khd->hqk/dot_general | solution.py:177
  307.4 17.8 %multiply_reduce_fusion = (f32[12,512]{1,0:T(8,128)S(1)}, f32[12,512,1024]{2,1,0:T(8,128)}) fusion(f32[12,512]{1,0:T(8,128)S(1)} %log_add_fusion, f32[12,512,1024]{2,1,0:T(8,128)} %get-tuple-element.85, pred[512,1024]{1,0:T(8,128)(4,1)S(1)} %copy-done.17, bf16[512,12,64]{0,2,1:T(8,128)(2,1)} %bitcast.80, bf16[1024,12,64]{0,2,1:T(8,128)(2,1)S(1)} %bitcast.71), kind=kOutput, calls=%fused_computation.1 | convolution fusion | flops 836757504 | bytes 53264384 | tf_op jit(solution)/shard_map/qhd,khd->hqk/dot_general | solution.py:177
  325.2 42.6 %multiply_convert_fusion = (bf16[12,512,1024]{2,1,0:T(8,128)(2,1)}, bf16[12,512,1024]{2,1,0:T(8,128)(2,1)}) fusion(f32[12,512,1024]{2,1,0:T(8,128)} %get-tuple-element.95, f32[12,512]{1,0:T(8,128)S(1)} %get-tuple-element.94, f32[12,512]{1,0:T(8,128)S(1)} %log_add_fusion, f32[12,512,1024]{2,1,0:T(8,128)} %get-tuple-element.85, ...), kind=kLoop, calls=%fused_computation | loop fusion | flops 75497472 | bytes 126976000 | tf_op jit(solution)/shard_map/convert_element_type | solution.py:181
  367.9 10.4 %convolution_multiply_fusion = f32[12,64,512]{2,1,0:T(8,128)} fusion(bf16[1024,12,64]{0,2,1:T(8,128)(2,1)} %copy-done.3, bf16[12,512,1024]{2,1,0:T(8,128)(2,1)} %get-tuple-element.100), kind=kOutput, calls=%fused_computation.99 | convolution fusion | flops 805699584 | bytes 15728640 | tf_op jit(solution)/shard_map/hqk,khd->qhd/dot_general | solution.py:183
  378.3 6.6 convolution_multiply_fusion.1
  384.9 2.3 maximum_multiply_fusion.3
  389.5 2.1 fusion.36
  391.6 2.3 fusion.55
  395.5 3.7 bitcast_multiply_fusion
  401.5 12.1 %fusion.4 = f32[12,64,1024]{2,1,0:T(8,128)S(1)} fusion(bf16[512,12,64]{0,2,1:T(8,128)(2,1)S(1)} %bitcast.81, f32[12,512]{1,0:T(8,128)S(1)} %log_add_fusion, f32[12,512,1024]{2,1,0:T(8,128)} %get-tuple-element.85, pred[512,1024]{1,0:T(8,128)(4,1)S(1)} %copy-done.18), kind=kOutput, calls=%fused_computation.16 | convolution fusion | flops 830472192 | bytes 29646848 | tf_op jit(solution)/shard_map/hqk,qhd->khd/dot_general | solution.py:174
  413.6 12.0 %add_convert_fusion.1 = bf16[12,64,1024]{2,1,0:T(8,128)(2,1)S(1)} fusion(f32[12,64,1024]{2,1,0:T(8,128)S(1)} %fusion.4, bf16[512,12,64]{0,2,1:T(8,128)(2,1)S(1)} %bitcast.79, f32[12,512]{1,0:T(8,128)S(1)} %log_add_fusion.1, f32[12,512,1024]{2,1,0:T(8,128)} %get-tuple-element.87, pred[512,1024]{1,0:T(8,128)(4,1)S(1)} %copy-done.15), kind=kOutput, calls=%fused_computation.78 | convolution fusion | flops 832045056 | bytes 31219712 | tf_op jit(solution)/shard_map/hqk,qhd->khd/dot_general | solution.py:174
  426.8 6.8 fusion.39
  436.1 13.5 %collective-permute-done = bf16[96,1152]{1,0:T(8,128)(2,1)} collective-permute-done((bf16[96,1152]{1,0:T(8,128)(2,1)S(1)}, bf16[96,1152]{1,0:T(8,128)(2,1)}, u32[]{:S(2)}, u32[]{:S(2)}) %collective-permute-start) | collective-permute-done | bytes 221216 | tf_op jit(solution)/shard_map/ppermute | solution.py:24
  450.5 14.0 %collective-permute-done.1 = bf16[96,1152]{1,0:T(8,128)(2,1)S(1)} collective-permute-done((bf16[96,1152]{1,0:T(8,128)(2,1)}, bf16[96,1152]{1,0:T(8,128)(2,1)S(1)}, u32[]{:S(2)}, u32[]{:S(2)}) %collective-permute-start.1) | collective-permute-done | bytes 221216 | tf_op jit(solution)/shard_map/ppermute | solution.py:24
  464.6 14.7 %collective-permute-done.2 = bf16[96,1152]{1,0:T(8,128)(2,1)S(1)} collective-permute-done((bf16[96,1152]{1,0:T(8,128)(2,1)S(1)}, bf16[96,1152]{1,0:T(8,128)(2,1)S(1)}, u32[]{:S(2)}, u32[]{:S(2)}) %collective-permute-start.2) | collective-permute-done | bytes 221216 | tf_op jit(solution)/shard_map/ppermute | solution.py:24
  479.3 14.2 %collective-permute-done.3 = bf16[96,1152]{1,0:T(8,128)(2,1)S(1)} collective-permute-done((bf16[96,1152]{1,0:T(8,128)(2,1)S(1)}, bf16[96,1152]{1,0:T(8,128)(2,1)S(1)}, u32[]{:S(2)}, u32[]{:S(2)}) %collective-permute-start.3) | collective-permute-done | bytes 221216 | tf_op jit(solution)/shard_map/ppermute | solution.py:24
  493.5 19.8 %collective-permute-done.4 = bf16[96,1152]{1,0:T(8,128)(2,1)S(1)} collective-permute-done((bf16[96,1152]{1,0:T(8,128)(2,1)S(1)}, bf16[96,1152]{1,0:T(8,128)(2,1)S(1)}, u32[]{:S(2)}, u32[]{:S(2)}) %collective-permute-start.4) | collective-permute-done | bytes 221216 | tf_op jit(solution)/shard_map/ppermute | solution.py:24
  513.4 8.7 %collective-permute-done.5 = bf16[96,1152]{1,0:T(8,128)(2,1)S(1)} collective-permute-done((bf16[96,1152]{1,0:T(8,128)(2,1)S(1)}, bf16[96,1152]{1,0:T(8,128)(2,1)S(1)}, u32[]{:S(2)}, u32[]{:S(2)}) %collective-permute-start.5) | collective-permute-done | bytes 221216 | tf_op jit(solution)/shard_map/ppermute | solution.py:24
  522.3 8.7 %collective-permute-done.6 = bf16[96,1152]{1,0:T(8,128)(2,1)S(1)} collective-permute-done((bf16[96,1152]{1,0:T(8,128)(2,1)S(1)}, bf16[96,1152]{1,0:T(8,128)(2,1)S(1)}, u32[]{:S(2)}, u32[]{:S(2)}) %collective-permute-start.6) | collective-permute-done | bytes 221216 | tf_op jit(solution)/shard_map/ppermute | solution.py:24
  531.0 5.5 fusion.30
  539.6 3.4 add_convert_fusion.2
  543.0 1.6 convert_element_type.166
  544.6 1.7 convert_element_type.170
  546.3 36.6 %reduce-scatter.9.cloned.1.call-done = f32[96,2304]{1,0:T(8,128)} async-done(((f32[768,2304]{1,0:T(8,128)}), f32[96,2304]{1,0:T(8,128)}) %reduce-scatter.9.cloned.1.call-update) | async-done | bytes 884752 | tf_op jit(solution)/shard_map/reduce_scatter | solution.py:212
  583.0 2.0 convert_element_type.168
  585.0 130.3 %reduce-scatter.5.cloned.1.call-done = f32[96,2304]{1,0:T(8,128)} async-done(((f32[768,2304]{1,0:T(8,128)}), f32[96,2304]{1,0:T(8,128)}) %reduce-scatter.5.cloned.1.call-update) | async-done | bytes 884752 | tf_op jit(solution)/shard_map/reduce_scatter | solution.py:210
  715.2 2.0 convert_element_type.164
  717.2 2.6 copy.55
  719.8 19.7 %all-reduce.6 = (bf16[768]{0:T(1024)(128)(2,1)S(1)}, bf16[768]{0:T(1024)(128)(2,1)S(1)}) all-reduce(f32[768]{0:T(1024)S(1)} %get-tuple-element.42, f32[768]{0:T(1024)S(1)} %copy-done.56), channel_id=6, replica_groups=mesh['fsdp'=8,'rep'=4] {'fsdp'}, use_global_device_ids=true, to_apply=%region_24.25.clone | all-reduce | flops 1536 | bytes 9216
  739.7 5.6 all-reduce.8
  746.3 6.1 add_add_fusion.2
  752.4 3.6 copy.56
  756.5 1.6 convert_element_type.167
  758.1 2.0 convert_element_type.165
  760.1 1.7 convert_element_type.171
  761.8 2.0 convert_element_type.169
  (229 shorter events, 45.1 us)
Async XLA Ops:
  7.2 36.7 %copy-start.34 = (bf16[1024,768]{1,0:T(8,128)(2,1)S(1)}, bf16[1024,768]{1,0:T(8,128)(2,1)}, u32[]{:S(2)}) copy-start(bf16[1024,768]{1,0:T(8,128)(2,1)} %param.10) | copy-start | bytes 4718596
  7.2 71.2 %all-gather.5.cloned.1.call-start = ((), (), s32[]{:S(2)}) async-start(), calls=%async_computation.4 | async-start | bytes 3981312 | tf_op jit(solution)/shard_map/all_gather | solution.py:90
  7.9 162.3 %all-gather.7.cloned.1.call-start = ((), (), s32[]{:S(2)}) async-start(), calls=%async_computation.5 | async-start | bytes 1327104 | tf_op jit(solution)/shard_map/all_gather | solution.py:91
  8.7 177.7 %all-gather.9.cloned.1.call-start = ((), (), s32[]{:S(2)}) async-start(), calls=%async_computation.6 | async-start | bytes 3981312 | tf_op jit(solution)/shard_map/all_gather | solution.py:92
  9.4 223.5 %all-gather.11.cloned.1.call-start = ((), (), s32[]{:S(2)}) async-start(), calls=%async_computation.7 | async-start | bytes 1990656 | tf_op jit(solution)/shard_map/all_gather | solution.py:137
  10.0 533.0 %reduce-scatter.7.cloned.1.call-start = ((), (), s32[]{:S(2)}) async-start(), calls=%async_computation.9 | async-start | bytes 2654208 | tf_op jit(solution)/shard_map/reduce_scatter | solution.py:211
  40.7 37.7 %copy-start.46 = (f32[768]{0:T(1024)}, f32[768]{0:T(1024)S(1)}, u32[]{:S(2)}) copy-start(f32[768]{0:T(1024)S(1)} %convert_element_type.135) | copy-start | bytes 9220
  43.9 57.2 %copy-start.29 = (f32[1024,64]{0,1:T(8,128)}, f32[1024,64]{0,1:T(8,128)S(1)}, u32[]{:S(2)}) copy-start(f32[1024,64]{0,1:T(8,128)S(1)} %get-tuple-element.77) | copy-start | bytes 786436
  44.7 125.6 %copy-start.1 = (bf16[1024,768]{0,1:T(8,128)(2,1)}, bf16[1024,768]{0,1:T(8,128)(2,1)S(1)}, u32[]{:S(2)}) copy-start(bf16[1024,768]{0,1:T(8,128)(2,1)S(1)} %copy.49) | copy-start | bytes 4718596
  44.7 3.6 copy-start.54
  45.0 39.6 %copy-start.42 = (f32[1024]{0:T(1024)}, f32[1024]{0:T(1024)S(1)}, u32[]{:S(2)}) copy-start(f32[1024]{0:T(1024)S(1)} %broadcast_multiply_fusion.4) | copy-start | bytes 12292
  46.6 38.0 %copy-start.48 = (f32[1024]{0:T(1024)}, f32[1024]{0:T(1024)S(1)}, u32[]{:S(2)}) copy-start(f32[1024]{0:T(1024)S(1)} %fusion.67) | copy-start | bytes 12292
  97.8 2.8 copy-start.5
  104.4 10.9 %copy-start.3 = (bf16[1024,12,64]{0,2,1:T(8,128)(2,1)}, bf16[1024,12,64]{0,2,1:T(8,128)(2,1)S(1)}, u32[]{:S(2)}) copy-start(bf16[1024,12,64]{0,2,1:T(8,128)(2,1)S(1)} %get-tuple-element.73) | copy-start | bytes 4718596
  104.4 10.9 %copy-start.7 = (bf16[1024,12,64]{0,2,1:T(8,128)(2,1)}, bf16[1024,12,64]{0,2,1:T(8,128)(2,1)S(1)}, u32[]{:S(2)}) copy-start(bf16[1024,12,64]{0,2,1:T(8,128)(2,1)S(1)} %get-tuple-element.72) | copy-start | bytes 4718596
  104.4 10.9 %copy-start.13 = (pred[512,1024]{1,0:T(8,128)(4,1)S(1)}, pred[512,1024]{1,0:T(8,128)(4,1)}, u32[]{:S(2)}) copy-start(pred[512,1024]{1,0:T(8,128)(4,1)} %get-tuple-element.78) | copy-start | bytes 1572868
  138.0 13.9 %slice-start = ((s8[25165824]{0:T(1024)(128)(4,1)}), s8[4194304]{0:T(1024)(128)(4,1)S(1)}, s32[]{:S(2)}) async-start(s8[25165824]{0:T(1024)(128)(4,1)} %bitcast.60), calls=%async_computation.13 | async-start | bytes 8388608
  138.0 13.9 %slice-start.1 = ((s8[25165824]{0:T(1024)(128)(4,1)}), s8[4194304]{0:T(1024)(128)(4,1)S(1)}, s32[]{:S(2)}) async-start(s8[25165824]{0:T(1024)(128)(4,1)} %bitcast.60), calls=%async_computation.14 | async-start | bytes 8388608
  138.0 13.8 %slice-start.2 = ((s8[25165824]{0:T(1024)(128)(4,1)}), s8[4194304]{0:T(1024)(128)(4,1)S(1)}, s32[]{:S(2)}) async-start(s8[25165824]{0:T(1024)(128)(4,1)} %bitcast.60), calls=%async_computation.15 | async-start | bytes 8388608
  138.0 13.8 %slice-start.3 = ((s8[25165824]{0:T(1024)(128)(4,1)}), s8[4194304]{0:T(1024)(128)(4,1)S(1)}, s32[]{:S(2)}) async-start(s8[25165824]{0:T(1024)(128)(4,1)} %bitcast.60), calls=%async_computation.16 | async-start | bytes 8388608
  138.1 14.7 %slice-start.4 = ((s8[25165824]{0:T(1024)(128)(4,1)}), s8[4194304]{0:T(1024)(128)(4,1)S(1)}, s32[]{:S(2)}) async-start(s8[25165824]{0:T(1024)(128)(4,1)} %bitcast.60), calls=%async_computation.17 | async-start | bytes 8388608
  138.1 16.2 %slice-start.5 = ((s8[25165824]{0:T(1024)(128)(4,1)}), s8[4194304]{0:T(1024)(128)(4,1)S(1)}, s32[]{:S(2)}) async-start(s8[25165824]{0:T(1024)(128)(4,1)} %bitcast.60), calls=%async_computation.18 | async-start | bytes 8388608
  173.5 12.9 %copy-start.55 = (f32[768]{0:T(1024)S(1)}, f32[768]{0:T(1024)}, u32[]{:S(2)}) copy-start(f32[768]{0:T(1024)} %convert_element_type.150) | copy-start | bytes 9220
  175.2 57.6 %copy-start.9 = (bf16[1024,768]{0,1:T(8,128)(2,1)S(1)}, bf16[1024,768]{0,1:T(8,128)(2,1)}, u32[]{:S(2)}) copy-start(bf16[1024,768]{0,1:T(8,128)(2,1)} %copy.54) | copy-start | bytes 4718596
  175.2 57.7 %copy-start.44 = (f32[1024]{0:T(1024)S(1)}, f32[1024]{0:T(1024)}, u32[]{:S(2)}) copy-start(f32[1024]{0:T(1024)} %convert_element_type.155) | copy-start | bytes 12292
  232.9 15.2 %copy-start.24 = (f32[1024,2304]{1,0:T(8,128)S(1)}, f32[1024,2304]{1,0:T(8,128)}, u32[]{:S(2)}) copy-start(f32[1024,2304]{1,0:T(8,128)} %fusion.83) | copy-start | bytes 28311556
  248.0 3.5 copy-start.20
  251.5 9.6 %copy-start.25 = (f32[1024,1152]{1,0:T(8,128)}, f32[1024,1152]{1,0:T(8,128)S(1)}, u32[]{:S(2)}) copy-start(f32[1024,1152]{1,0:T(8,128)S(1)} %get-tuple-element.58) | copy-start | bytes 14155780
  267.6 277.0 %reduce-scatter.11.cloned.1.call-start = ((), (), s32[]{:S(2)}) async-start(), calls=%async_computation.11 | async-start | bytes 3981312 | tf_op jit(solution)/shard_map/reduce_scatter | solution.py:213
  273.4 4.7 slice-start.9
  273.4 309.6 %reduce-scatter.9.cloned.1.call-start = ((), (), s32[]{:S(2)}) async-start(), calls=%async_computation.10 | async-start | bytes 7962624 | tf_op jit(solution)/shard_map/reduce_scatter | solution.py:212
  273.5 4.6 slice-start.10
  288.4 426.8 %reduce-scatter.5.cloned.1.call-start = ((), (), s32[]{:S(2)}) async-start(), calls=%async_computation.8 | async-start | bytes 7962624 | tf_op jit(solution)/shard_map/reduce_scatter | solution.py:210
  289.5 18.0 %copy-start.17 = (pred[512,1024]{1,0:T(8,128)(4,1)S(1)}, pred[512,1024]{1,0:T(8,128)(4,1)}, u32[]{:S(2)}) copy-start(pred[512,1024]{1,0:T(8,128)(4,1)} %get-tuple-element.79) | copy-start | bytes 1572868
  367.9 10.4 %copy-start = (bf16[12,512,1024]{2,1,0:T(8,128)(2,1)S(1)}, bf16[12,512,1024]{2,1,0:T(8,128)(2,1)}, u32[]{:S(2)}) copy-start(bf16[12,512,1024]{2,1,0:T(8,128)(2,1)} %get-tuple-element.101) | copy-start | bytes 37748740
  378.3 6.6 copy-start.32
  389.5 4.4 slice-start.6
  391.6 3.9 slice-start.8
  391.6 3.9 copy-start.28
  401.5 24.1 %copy-start.38 = (bf16[1024,12,64]{0,2,1:T(8,128)(2,1)}, bf16[1024,12,64]{0,2,1:T(8,128)(2,1)S(1)}, u32[]{:S(2)}) copy-start(bf16[1024,12,64]{0,2,1:T(8,128)(2,1)S(1)} %fusion.37) | copy-start | bytes 4718596
  401.5 12.1 %copy-start.15 = (pred[512,1024]{1,0:T(8,128)(4,1)S(1)}, pred[512,1024]{1,0:T(8,128)(4,1)}, u32[]{:S(2)}) copy-start(pred[512,1024]{1,0:T(8,128)(4,1)} %get-tuple-element.78) | copy-start | bytes 1572868
  401.5 12.1 %copy-start.26 = (bf16[512,768]{0,1:T(8,128)(2,1)S(1)}, bf16[512,768]{0,1:T(8,128)(2,1)}, u32[]{:S(2)}) copy-start(bf16[512,768]{0,1:T(8,128)(2,1)} %get-tuple-element.70) | copy-start | bytes 2359300
  413.6 13.2 %copy-start.2 = (bf16[1024,768]{0,1:T(8,128)(2,1)S(1)}, bf16[1024,768]{0,1:T(8,128)(2,1)}, u32[]{:S(2)}) copy-start(bf16[1024,768]{0,1:T(8,128)(2,1)} %copy-done.1) | copy-start | bytes 4718596
  413.6 13.2 %copy-start.37 = (bf16[1024,768]{0,1:T(8,128)(2,1)S(1)}, bf16[1024,768]{0,1:T(8,128)(2,1)}, u32[]{:S(2)}) copy-start(bf16[1024,768]{0,1:T(8,128)(2,1)} %fusion.36) | copy-start | bytes 4718596
  413.6 13.2 %copy-start.43 = (f32[1024]{0:T(1024)S(1)}, f32[1024]{0:T(1024)}, u32[]{:S(2)}) copy-start(f32[1024]{0:T(1024)} %copy-done.42) | copy-start | bytes 12292
  413.6 13.2 %copy-start.47 = (f32[768]{0:T(1024)S(1)}, f32[768]{0:T(1024)}, u32[]{:S(2)}) copy-start(f32[768]{0:T(1024)} %copy-done.46) | copy-start | bytes 9220
  413.6 13.2 %copy-start.49 = (f32[1024]{0:T(1024)S(1)}, f32[1024]{0:T(1024)}, u32[]{:S(2)}) copy-start(f32[1024]{0:T(1024)} %copy-done.48) | copy-start | bytes 12292
  433.6 322.9 %all-reduce.12.cloned.1.call-start = ((), (), s32[]{:S(2)}) async-start(), calls=%async_computation.12 | async-start | bytes 2506752 | tf_op jit(solution)/shard_map/psum | solution.py:218
  434.5 15.0 %collective-permute-start = (bf16[96,1152]{1,0:T(8,128)(2,1)S(1)}, bf16[96,1152]{1,0:T(8,128)(2,1)}, u32[]{:S(2)}, u32[]{:S(2)}) collective-permute-start(bf16[96,1152]{1,0:T(8,128)(2,1)S(1)} %copy-done.41), channel_id=1, source_target_pairs={{0,4},{4,8},{8,12},{12,16},{16,20},{20,24},{24,28},{28,0},{1,5},{5... | collective-permute-start | bytes 663560 | tf_op jit(solution)/shard_map/ppermute | solution.py:24
  435.9 95.1 %copy-start.39 = (bf16[1024,12,64]{0,2,1:T(8,128)(2,1)S(1)}, bf16[1024,12,64]{0,2,1:T(8,128)(2,1)}, u32[]{:S(2)}) copy-start(bf16[1024,12,64]{0,2,1:T(8,128)(2,1)} %copy-done.38) | copy-start | bytes 4718596
  435.9 95.1 %copy-start.57 = (bf16[768,2304]{1,0:T(8,128)(2,1)S(1)}, bf16[768,2304]{1,0:T(8,128)(2,1)}, u32[]{:S(2)}) copy-start(bf16[768,2304]{1,0:T(8,128)(2,1)} %all-gather.5.cloned.1.call-done) | copy-start | bytes 10616836
  449.5 15.0 %collective-permute-start.1 = (bf16[96,1152]{1,0:T(8,128)(2,1)}, bf16[96,1152]{1,0:T(8,128)(2,1)S(1)}, u32[]{:S(2)}, u32[]{:S(2)}) collective-permute-start(bf16[96,1152]{1,0:T(8,128)(2,1)} %collective-permute-done), channel_id=1, source_target_pairs={{0,4},{4,8},{8,12},{12,16},{16,20},{20,24},{24,28},{28,0},{1,5},{5... | collective-permute-start | bytes 663560 | tf_op jit(solution)/shard_map/ppermute | solution.py:24
  464.6 14.7 %collective-permute-start.2 = (bf16[96,1152]{1,0:T(8,128)(2,1)S(1)}, bf16[96,1152]{1,0:T(8,128)(2,1)S(1)}, u32[]{:S(2)}, u32[]{:S(2)}) collective-permute-start(bf16[96,1152]{1,0:T(8,128)(2,1)S(1)} %collective-permute-done.1), channel_id=1, source_target_pairs={{0,4},{4,8},{8,12},{12,16},{16,20},{20,24},{24,28},{28,0},{1,5},{5... | collective-permute-start | bytes 663560 | tf_op jit(solution)/shard_map/ppermute | solution.py:24
  479.3 14.2 %collective-permute-start.3 = (bf16[96,1152]{1,0:T(8,128)(2,1)S(1)}, bf16[96,1152]{1,0:T(8,128)(2,1)S(1)}, u32[]{:S(2)}, u32[]{:S(2)}) collective-permute-start(bf16[96,1152]{1,0:T(8,128)(2,1)S(1)} %collective-permute-done.2), channel_id=1, source_target_pairs={{0,4},{4,8},{8,12},{12,16},{16,20},{20,24},{24,28},{28,0},{1,5},{5... | collective-permute-start | bytes 663560 | tf_op jit(solution)/shard_map/ppermute | solution.py:24
  493.5 19.9 %collective-permute-start.4 = (bf16[96,1152]{1,0:T(8,128)(2,1)S(1)}, bf16[96,1152]{1,0:T(8,128)(2,1)S(1)}, u32[]{:S(2)}, u32[]{:S(2)}) collective-permute-start(bf16[96,1152]{1,0:T(8,128)(2,1)S(1)} %collective-permute-done.3), channel_id=1, source_target_pairs={{0,4},{4,8},{8,12},{12,16},{16,20},{20,24},{24,28},{28,0},{1,5},{5... | collective-permute-start | bytes 663560 | tf_op jit(solution)/shard_map/ppermute | solution.py:24
  513.3 8.7 %collective-permute-start.5 = (bf16[96,1152]{1,0:T(8,128)(2,1)S(1)}, bf16[96,1152]{1,0:T(8,128)(2,1)S(1)}, u32[]{:S(2)}, u32[]{:S(2)}) collective-permute-start(bf16[96,1152]{1,0:T(8,128)(2,1)S(1)} %collective-permute-done.4), channel_id=1, source_target_pairs={{0,4},{4,8},{8,12},{12,16},{16,20},{20,24},{24,28},{28,0},{1,5},{5... | collective-permute-start | bytes 663560 | tf_op jit(solution)/shard_map/ppermute | solution.py:24
  522.1 8.9 %collective-permute-start.6 = (bf16[96,1152]{1,0:T(8,128)(2,1)S(1)}, bf16[96,1152]{1,0:T(8,128)(2,1)S(1)}, u32[]{:S(2)}, u32[]{:S(2)}) collective-permute-start(bf16[96,1152]{1,0:T(8,128)(2,1)S(1)} %collective-permute-done.5), channel_id=1, source_target_pairs={{0,4},{4,8},{8,12},{12,16},{16,20},{20,24},{24,28},{28,0},{1,5},{5... | collective-permute-start | bytes 663560 | tf_op jit(solution)/shard_map/ppermute | solution.py:24
  531.0 5.5 copy-start.53
  531.0 8.5 %copy-start.33 = (bf16[1024,1152]{1,0:T(8,128)(2,1)S(1)}, bf16[1024,1152]{1,0:T(8,128)(2,1)}, u32[]{:S(2)}) copy-start(bf16[1024,1152]{1,0:T(8,128)(2,1)} %get-tuple-element.59) | copy-start | bytes 7077892
  536.5 3.1 copy-start.22
  584.9 134.9 %copy-start.56 = (f32[768]{0:T(1024)S(1)}, f32[768]{0:T(1024)}, u32[]{:S(2)}) copy-start(f32[768]{0:T(1024)} %get-tuple-element.40) | copy-start | bytes 9220
  584.9 161.4 %copy-start.10 = (bf16[1024,768]{0,1:T(8,128)(2,1)S(1)}, bf16[1024,768]{0,1:T(8,128)(2,1)}, u32[]{:S(2)}) copy-start(bf16[1024,768]{0,1:T(8,128)(2,1)} %copy.54) | copy-start | bytes 4718596
  585.0 161.4 %copy-start.45 = (f32[1024]{0:T(1024)S(1)}, f32[1024]{0:T(1024)}, u32[]{:S(2)}) copy-start(f32[1024]{0:T(1024)} %convert_element_type.155) | copy-start | bytes 12292
  585.0 161.4 %copy-start.51 = (f32[1024]{0:T(1024)S(1)}, f32[1024]{0:T(1024)}, u32[]{:S(2)}) copy-start(f32[1024]{0:T(1024)} %copy-done.50) | copy-start | bytes 12292
  (24 other events, 41.0 us)
Sparse Core Ops, SparseCore 0:
  10.2 68.1 all-gather.4
  80.6 39.5 all-gather.6
  122.4 63.9 all-gather.8
  188.4 44.3 all-gather.10
  267.8 68.0 reduce-scatter.6
  339.3 78.1 reduce-scatter.10
  421.2 161.7 reduce-scatter.8
  587.1 128.0 reduce-scatter.4
  718.4 38.0 all-reduce.11
